TPU v7x, 256 devices: a whole 4x4x8 slice. The times are simulated.
256 devices in a mesh: dp: 4 (over x), seq: 16 (over z, core), mp: 4 (over y).
Axes of the slice: x: 4, y: 4, z: 8, core: 2. Of those that a mesh axis runs over, the one named last changes fastest.
Arguments:
- patches: bfloat16 [16384, 3072], P(('dp', 'seq'), 'mp'), may hold values from -20 to 20
- image_of: int32 [16384], P(('dp', 'seq')), may hold values from 0 to 31, as said below
- prompt_of: int32 [4, 32], P('dp', 'seq'), may hold values from 0 to 15
- text_len: int32 [4, 16], P('dp'), may hold values from 1 to 256, as said below
- text_kv: bfloat16 [64, 256, 2, 1536], P('dp', 'seq', None, 'mp'), may hold values from -70 to 70
- w_qkv: bfloat16 [3072, 3, 1536], P(None, None, 'mp'), may hold values from -0.109375 to 0.109375
- w_out: bfloat16 [1536, 3072], P('mp'), may hold values from -0.15625 to 0.15625
- pre_gain: float32 [3072], replicated, may hold values from 0.1 to 1.9
- pre_bias: float32 [3072], replicated, may hold values from -3 to 3
- post_gain: float32 [3072], replicated, may hold values from 0.1 to 1.9
- post_bias: float32 [3072], replicated, may hold values from -3 to 3
Outputs:
- block_out: bfloat16 [16384, 3072], P(('dp', 'seq'), 'mp')
Inputs may be any that keep to these rules, and one draw needn't show every extreme that they name: `image_of`: the rows of one device name each image at most 16 times; in every data-parallel group one image is named exactly 16 times by the rows of every device of that group. `text_len`: in every data-parallel group some prompt has all 256 tokens live.
All inputs are finite; a program needn't handle non-finite values.
Results may differ from a plain program's by a relative error of at most 0.011.
Values may be sent and summed in bfloat16 or wider, within the bound.
A program may use at most 128 MiB of HBM per device.

v0:
```python
import math
import jax
import jax.numpy as jnp
from jax import lax
from jax.sharding import PartitionSpec as P

HD = 128
epsilon = 1e-05


def layer_norm(values_in, gain_vec, bias_vec):
    average = jnp.mean(values_in, axis=-1, keepdims=True)
    centered = values_in - average
    spread = jnp.mean(centered * centered, axis=-1, keepdims=True)
    return centered * lax.rsqrt(spread + epsilon) * gain_vec + bias_vec


def slot_layout(image_of, local_images, seq_count):
    tok_rows = image_of.shape[0]
    images_all = local_images * seq_count
    slot_depth = 2 * tok_rows // images_all
    slot_span = seq_count * slot_depth
    onehot = (image_of[:, None] == jnp.arange(images_all, dtype=jnp.int32)[None, :]).astype(
        jnp.int32
    )
    ranking = jnp.sum(jnp.cumsum(onehot, axis=0) * onehot, axis=1) - 1
    owner_index = image_of // local_images
    within = image_of % local_images
    position = within * slot_span + owner_index * slot_depth + ranking
    total_slots = local_images * slot_span
    source_row = (
        jnp.zeros((total_slots,), jnp.int32).at[position].set(jnp.arange(tok_rows, dtype=jnp.int32))
    )
    filled = (
        jnp.zeros((total_slots,), jnp.bfloat16)
        .at[position]
        .set(jnp.ones((tok_rows,), jnp.bfloat16))
    )
    return (position, source_row, filled, slot_span)


def dispatch(row_data, layout, local_images):
    position, source_row, filled, slot_span = layout
    buffer = jnp.take(row_data, source_row, axis=0) * filled[:, None]
    buffer = buffer.reshape(local_images, slot_span, row_data.shape[1])
    return (
        lax.all_to_all(buffer, "seq", split_axis=1, concat_axis=1, tiled=True),
        lax.all_to_all(
            filled.reshape(local_images, slot_span), "seq", split_axis=1, concat_axis=1, tiled=True
        ),
    )


def collect(slot_data, layout):
    position = layout[0]
    returned = lax.all_to_all(slot_data, "seq", split_axis=1, concat_axis=1, tiled=True)
    return jnp.take(returned.reshape(-1, slot_data.shape[2]), position, axis=0)


def project(row_data, w_qkv, pre_gain, pre_bias):
    gathered = lax.all_gather(row_data, "mp", axis=1, tiled=True)
    normed = layer_norm(gathered.astype(jnp.float32), pre_gain, pre_bias).astype(jnp.bfloat16)
    merged = w_qkv.reshape(w_qkv.shape[0], -1)
    return jnp.dot(normed, merged, preferred_element_type=jnp.float32).astype(jnp.bfloat16)


def attend(projected, filled, prompts, chosen, lengths):
    image_count, slot_span, triple = projected.shape
    head_cols = triple // 3
    head_count = head_cols // HD
    softmax_scale = 1.0 / math.sqrt(HD)
    queries = projected[:, :, :head_cols].reshape(image_count, slot_span, head_count, HD)
    image_key_rows = projected[:, :, head_cols : 2 * head_cols].reshape(
        image_count, slot_span, head_count, HD
    )
    vals_img = projected[:, :, 2 * head_cols :].reshape(image_count, slot_span, head_count, HD)
    txt_len = chosen.shape[1]
    keys_txt = chosen[:, :, 0].reshape(image_count, txt_len, head_count, HD)
    vals_txt = chosen[:, :, 1].reshape(image_count, txt_len, head_count, HD)
    prompt_count = lengths.shape[0]
    prompt_match = prompts[:, None] == jnp.arange(prompt_count, dtype=jnp.int32)[None, :]
    image_len = jnp.sum(jnp.where(prompt_match, lengths[None, :], 0), axis=1)
    token_live = jnp.arange(txt_len, dtype=jnp.int32)[None, :] < image_len[:, None]
    image_score_matrix = (
        jnp.einsum("ilhd,imhd->ihlm", queries, image_key_rows, preferred_element_type=jnp.float32)
        * softmax_scale
    )
    image_score_matrix = jnp.where((filled > 0)[:, None, None, :], image_score_matrix, -jnp.inf)
    scores_txt = (
        jnp.einsum("ilhd,ithd->ihlt", queries, keys_txt, preferred_element_type=jnp.float32)
        * softmax_scale
    )
    scores_txt = jnp.where(token_live[:, None, None, :], scores_txt, -jnp.inf)
    scores = jnp.concatenate([image_score_matrix, scores_txt], axis=-1)
    highest = jnp.max(scores, axis=-1, keepdims=True)
    exponent = jnp.exp(scores - highest)
    attention_probs = (exponent / jnp.sum(exponent, axis=-1, keepdims=True)).astype(jnp.bfloat16)
    joint_value_rows = jnp.concatenate([vals_img, vals_txt], axis=1)
    mixed_output = jnp.einsum(
        "ihlm,imhd->ilhd", attention_probs, joint_value_rows, preferred_element_type=jnp.float32
    )
    return mixed_output.astype(jnp.bfloat16).reshape(image_count, slot_span, head_cols)


def finish(attended, residual, w_out, post_gain, post_bias):
    partial_sum = jnp.dot(attended, w_out, preferred_element_type=jnp.float32)
    share_cols = residual.shape[1]
    full_cols = partial_sum.shape[1]
    offset = lax.axis_index("mp") * share_cols
    gain_part = lax.dynamic_slice_in_dim(post_gain, offset, share_cols)
    bias_part = lax.dynamic_slice_in_dim(post_bias, offset, share_cols)
    owned_part = lax.psum_scatter(partial_sum, "mp", scatter_dimension=1, tiled=True)
    totals = lax.psum((jnp.sum(owned_part, axis=1), jnp.sum(owned_part * owned_part, axis=1)), "mp")
    average = (totals[0] / full_cols)[:, None]
    spread = (totals[1] / full_cols)[:, None] - average * average
    normed = (owned_part - average) * lax.rsqrt(spread + epsilon) * gain_part + bias_part
    return (residual.astype(jnp.float32) + normed).astype(jnp.bfloat16)


def shards(
    patches,
    image_of,
    prompt_of,
    text_len,
    text_kv,
    w_qkv,
    w_out,
    pre_gain,
    pre_bias,
    post_gain,
    post_bias,
):
    seq_count = lax.axis_size("seq")
    local_images = prompt_of.shape[1]
    layout = slot_layout(image_of, local_images, seq_count)
    slot_span = layout[3]
    prompts = prompt_of[0]
    lengths = text_len[0]
    text_all = lax.all_gather(text_kv, "seq", axis=1, tiled=True)
    chosen = jnp.take(text_all, prompts, axis=0)
    arrived, filled = dispatch(patches, layout, local_images)
    slot_rows = arrived.reshape(local_images * slot_span, arrived.shape[2])
    projected = project(slot_rows, w_qkv, pre_gain, pre_bias)
    attended = attend(
        projected.reshape(local_images, slot_span, -1), filled, prompts, chosen, lengths
    )
    finished = finish(
        attended.reshape(local_images * slot_span, -1), slot_rows, w_out, post_gain, post_bias
    )
    result = collect(finished.reshape(local_images, slot_span, -1), layout)
    return result


def solution(mesh):
    placed = (
        P(("dp", "seq"), "mp"),
        P(("dp", "seq")),
        P("dp", "seq"),
        P("dp", None),
        P("dp", "seq", None, "mp"),
        P(None, None, "mp"),
        P("mp", None),
        P(),
        P(),
        P(),
        P(),
    )
    return jax.shard_map(
        shards, mesh=mesh, in_specs=placed, out_specs=P(("dp", "seq"), "mp"), check_vma=False
    )
```

profile of v0, /device:TPU:1, one launch (start us, length us, event | category | flops | bytes accessed | tf_op | source)
XLA Modules:
  0.0 273.3 jit_solution(16353884575686637461)
XLA Ops:
  9.0 1.2 compare_and_fusion.2
  10.2 1.4 scatter_custom_fusion
  11.6 2.2 scatter_custom_fusion.1
  14.2 3.4 %gather_fusion = bf16[512,768]{1,0:T(8,128)(2,1)S(1)} fusion(bf16[256,768]{1,0:T(8,128)(2,1)} %param.11, s32[1024]{0:T(1024)S(1)} %pad_clamp_fusion.2), kind=kCustom, calls=%fused_computation | custom fusion | bytes 1574912 | tf_op jit(solution)/shard_map/jit(_take)/gather | solution.py:44
  17.6 1.6 fusion.20
  19.3 32.8 %all_to_all.19 = bf16[2,256,768]{2,0,1:T(2,128)(2,1)S(1)} all-to-all(bf16[2,256,768]{2,0,1:T(2,128)(2,1)S(1)} %fusion.20), channel_id=1, replica_groups=mesh['dp'=4,'seq'=16,'mp'=4] {'seq'}, dimensions={1} | all-to-all | bytes 1572864 | tf_op jit(solution)/shard_map/all_to_all | solution.py:47
  52.1 1.0 copy.84
  54.7 3.4 %all-to-all-start.1 = ((bf16[2,16,16]{2,0,1:T(2,128)(2,1)}), bf16[2,16,16]{2,0,1:T(2,128)(2,1)S(1)}, u32[]{:S(2)}, u32[]{:S(2)}) async-start(bf16[2,16,16]{2,0,1:T(2,128)(2,1)} %copy.89), calls=%async_computation.1 | async-start | bytes 16384 | tf_op jit(solution)/shard_map/all_to_all | solution.py:48
  59.8 10.4 %copy.85 = bf16[3072,3,384]{0,2,1:T(8,128)(2,1)} copy(bf16[3072,3,384]{2,0,1:T(8,128)(2,1)} %param.16) | data formatting | bytes 14155776 | tf_op args[5]
  70.3 21.8 %all-gather.3.cloned.1.call-done = bf16[512,3072]{1,0:T(8,128)(2,1)} async-done(((bf16[512,768]{1,0:T(8,128)(2,1)}), bf16[512,3072]{1,0:T(8,128)(2,1)}) %all-gather.3.cloned.1.call-update) | async-done | bytes 3145744 | tf_op jit(solution)/shard_map/all_gather | solution.py:61
  92.1 2.5 convert_reduce_fusion
  94.9 1.0 fusion.2
  95.9 7.7 %fusion.13 = bf16[512,1152]{1,0:T(8,128)(2,1)S(1)} fusion(bf16[3072,1152]{0,1:T(8,128)(2,1)} %bitcast.50, bf16[512,3072]{1,0:T(8,128)(2,1)S(1)} %copy-done.1, f32[3072]{0:T(1024)S(1)} %copy-done.10, f32[3072]{0:T(1024)S(1)} %copy-done.11, f32[512]{0:T(512)S(1)} %add_rsqrt_fusion.1, f32[512]{0:T(512)S(1)} %broadcast_multiply_fusion.1), kind=kOutput, calls=%fused_computation.21 | convolution fusion | flops 3633905664 | bytes 11431936 | tf_op jit(solution)/shard_map/dot_general | solution.py:64
  103.6 0.9 fusion.39
  104.5 1.2 copy.107
  105.7 0.9 copy.108
  106.6 1.0 copy.86
  107.6 2.6 fusion.41
  110.1 30.5 %all-gather.5.cloned.1.call-done = bf16[16,256,2,384]{3,1,2,0:T(8,128)(2,1)} async-done(((bf16[16,16,2,384]{3,1,2,0:T(8,128)(2,1)}), bf16[16,256,2,384]{3,1,2,0:T(8,128)(2,1)}) %all-gather.5.cloned.1.call-update) | async-done | bytes 6291472 | tf_op jit(solution)/shard_map/all_gather | solution.py:139
  140.7 3.5 %gather_fusion.1 = bf16[2,256,2,384]{3,1,2,0:T(8,128)(2,1)S(1)} fusion(bf16[16,256,2,384]{3,1,2,0:T(8,128)(2,1)} %all-gather.5.cloned.1.call-done, s32[1024]{0:T(1024)S(1)} %pad_clamp_fusion.1), kind=kCustom, calls=%fused_computation.1 | custom fusion | bytes 1572872 | tf_op jit(solution)/shard_map/jit(_take)/gather | solution.py:140
  145.1 0.9 copy.95
  146.3 1.6 fusion.42
  149.5 4.5 %fusion.43 = f32[512,3072]{1,0:T(8,128)} fusion(bf16[512,384]{0,1:T(8,128)(2,1)S(1)} %bitcast.56, bf16[384,3072]{1,0:T(8,128)(2,1)S(1)} %copy-done), kind=kOutput, calls=%fused_computation.83 | convolution fusion | flops 1207959552 | bytes 9043968 | tf_op jit(solution)/shard_map/dot_general | solution.py:106
  155.7 63.3 %reduce-scatter.2.cloned.1.call-done = f32[512,768]{1,0:T(8,128)} async-done(((f32[512,3072]{1,0:T(8,128)}), f32[512,768]{1,0:T(8,128)}) %reduce-scatter.2.cloned.1.call-update) | async-done | bytes 1572880 | tf_op jit(solution)/shard_map/reduce_scatter | solution.py:112
  219.0 1.7 fusion.38
  220.7 6.8 %all-reduce = (f32[512]{0:T(512)S(1)}, f32[512]{0:T(512)S(1)}) all-reduce(f32[512]{0:T(512)S(1)} %get-tuple-element.6, f32[512]{0:T(512)S(1)} %get-tuple-element.5), channel_id=1, replica_groups=mesh['dp'=4,'seq'=16,'mp'=4] {'mp'}, use_global_device_ids=true, to_apply=%region_15.16 | all-reduce | flops 1024 | bytes 8192 | tf_op jit(solution)/shard_map/psum | solution.py:113
  227.5 1.8 add_convert_fusion
  229.3 1.7 copy.100
  231.0 9.7 %all-to-all-start.2 = ((bf16[2,256,768]{2,0,1:T(2,128)(2,1)}), bf16[2,256,768]{2,0,1:T(2,128)(2,1)}, u32[]{:S(2)}, u32[]{:S(2)}) async-start(bf16[2,256,768]{2,0,1:T(2,128)(2,1)} %copy.100), calls=%async_computation.3 | async-start | bytes 1572864 | tf_op jit(solution)/shard_map/all_to_all | solution.py:56
  240.7 22.7 %all-to-all-done.2 = bf16[2,256,768]{2,0,1:T(2,128)(2,1)} async-done(((bf16[2,256,768]{2,0,1:T(2,128)(2,1)}), bf16[2,256,768]{2,0,1:T(2,128)(2,1)}, u32[]{:S(2)}, u32[]{:S(2)}) %all-to-all-start.2) | async-done | bytes 786464 | tf_op jit(solution)/shard_map/all_to_all | solution.py:56
  263.5 1.2 copy.101
  264.7 1.2 gather_fusion.2
  (76 shorter events, 11.7 us)
Async XLA Ops:
  6.5 143.0 %copy-start = (bf16[384,3072]{1,0:T(8,128)(2,1)S(1)}, bf16[384,3072]{1,0:T(8,128)(2,1)}, u32[]{:S(2)}) copy-start(bf16[384,3072]{1,0:T(8,128)(2,1)} %param.17) | copy-start | bytes 7077892
  6.5 85.6 %all-gather.3.cloned.1.call-start = ((), (), s32[]{:S(2)}) async-start(), calls=%async_computation.4 | async-start | bytes 3932160 | tf_op jit(solution)/shard_map/all_gather | solution.py:61
  10.2 3.8 %copy-start.6 = (s32[256]{0:T(256)}, s32[256]{0:T(256)S(1)}, u32[]{:S(2)}) copy-start(s32[256]{0:T(256)S(1)} %get-tuple-element.10) | copy-start | bytes 3076
  19.3 33.9 %copy-start.4 = (bf16[16,16,2,384]{3,2,1,0:T(2,128)(2,1)S(1)}, bf16[16,16,2,384]{3,2,1,0:T(2,128)(2,1)}, u32[]{:S(2)}) copy-start(bf16[16,16,2,384]{3,2,1,0:T(2,128)(2,1)} %param.15) | copy-start | bytes 1179652
  19.3 39.1 %copy-start.12 = (s32[1,16]{1,0:T(1,128)S(1)}, s32[1,16]{1,0:T(1,128)}, u32[]{:S(2)}) copy-start(s32[1,16]{1,0:T(1,128)} %param.14) | copy-start | bytes 196
  19.3 39.1 %copy-start.13 = (s32[1,2]{1,0:T(1,128)S(1)}, s32[1,2]{1,0:T(1,128)}, u32[]{:S(2)}) copy-start(s32[1,2]{1,0:T(1,128)} %param.13) | copy-start | bytes 28
  53.1 87.5 %all-gather.5.cloned.1.call-start = ((), (), s32[]{:S(2)}) async-start(), calls=%async_computation.5 | async-start | bytes 6684672 | tf_op jit(solution)/shard_map/all_gather | solution.py:139
  54.7 15.4 %all-to-all-start.1 = ((bf16[2,16,16]{2,0,1:T(2,128)(2,1)}), bf16[2,16,16]{2,0,1:T(2,128)(2,1)S(1)}, u32[]{:S(2)}, u32[]{:S(2)}) async-start(bf16[2,16,16]{2,0,1:T(2,128)(2,1)} %copy.89), calls=%async_computation.1 | async-start | bytes 16384 | tf_op jit(solution)/shard_map/all_to_all | solution.py:48
  58.1 160.9 %reduce-scatter.2.cloned.1.call-start = ((), (), s32[]{:S(2)}) async-start(), calls=%async_computation.6 | async-start | bytes 7864320 | tf_op jit(solution)/shard_map/reduce_scatter | solution.py:112
  92.1 2.8 %copy-start.1 = (bf16[512,3072]{1,0:T(8,128)(2,1)S(1)}, bf16[512,3072]{1,0:T(8,128)(2,1)}, u32[]{:S(2)}) copy-start(bf16[512,3072]{1,0:T(8,128)(2,1)} %all-gather.3.cloned.1.call-done) | copy-start | bytes 9437188
  94.6 1.3 copy-start.10
  94.6 1.3 copy-start.11
  144.2 2.1 copy-start.9
  146.2 1.6 copy-start.3
  146.2 2.0 copy-start.5
  154.0 73.4 %copy-start.2 = (bf16[2,256,768]{2,1,0:T(8,128)(2,1)S(1)}, bf16[2,256,768]{2,1,0:T(8,128)(2,1)}, u32[]{:S(2)}) copy-start(bf16[2,256,768]{2,1,0:T(8,128)(2,1)} %copy.84) | copy-start | bytes 2359300
  229.3 11.4 %copy-start.7 = (s32[256]{0:T(256)S(1)}, s32[256]{0:T(256)}, u32[]{:S(2)}) copy-start(s32[256]{0:T(256)} %copy-done.6) | copy-start | bytes 3076
  231.0 32.4 %all-to-all-start.2 = ((bf16[2,256,768]{2,0,1:T(2,128)(2,1)}), bf16[2,256,768]{2,0,1:T(2,128)(2,1)}, u32[]{:S(2)}, u32[]{:S(2)}) async-start(bf16[2,256,768]{2,0,1:T(2,128)(2,1)} %copy.100), calls=%async_computation.3 | async-start | bytes 1572864 | tf_op jit(solution)/shard_map/all_to_all | solution.py:56
  240.7 25.2 %copy-start.8 = (pred[256]{0:T(512)(128)(4,1)S(1)}, pred[256]{0:T(512)(128)(4,1)}, u32[]{:S(2)}) copy-start(pred[256]{0:T(512)(128)(4,1)} %get-tuple-element.9) | copy-start | bytes 772
Sparse Core Ops, SparseCore 0:
  53.3 38.7 all-gather.2
  94.0 46.6 all-gather.4
  154.2 64.7 reduce-scatter.1
where the time goes:
time: 274 us; the launch traced here: 273 us
  waiting for transfers between devices  138 us (50%)
  blocking collectives  39.6 us (14%)
  local copies, waits for them, and re-layouts  35.6 us (13%)
  matrix products  17.1 us (6%)
  other arithmetic  15.7 us (6%)
  between operations  13.5 us (5%)
  starting transfers between devices  13.3 us (5%)
    reduce_scatter x1, waiting for transfers between devices, finish(): lax.psum_scatter(partial_sum, 'mp', scatter_dimension=1, tiled=True)  63.3 us
    all_to_all x1, blocking collectives, dispatch(): lax.all_to_all(buffer, 'seq', split_axis=1, concat_axis=1, tiled=True)  32.8 us
    all_gather x1, waiting for transfers between devices, shards(): text_all = lax.all_gather(text_kv, 'seq', axis=1, tiled=True)  30.5 us
    all_to_all x1, waiting for transfers between devices, collect(): lax.all_to_all(slot_data, 'seq', split_axis=1, concat_axis=1, tiled=True)  22.7 us
    all_gather x1, waiting for transfers between devices, project(): gathered = lax.all_gather(row_data, 'mp', axis=1, tiled=True)  21.8 us
    unnamed x33, local copies, waits for them, and re-layouts  13.7 us
    all_to_all x1, starting transfers between devices, collect(): lax.all_to_all(slot_data, 'seq', split_axis=1, concat_axis=1, tiled=True)  9.67 us
    dot_general x1, matrix products, project(): jnp.dot(normed, merged, preferred_element_type=jnp.float32)  7.7 us
  transfers between devices with their start and end apart: 5, of which 4 were waited for; matrix products, arithmetic and copies ran while one was open for 12% of the time, Pallas kernels for 0%

commit v1 on v0

--- a/solution.py
+++ b/solution.py
@@ -136,7 +136,9 @@
     slot_span = layout[3]
     prompts = prompt_of[0]
     lengths = text_len[0]
-    text_all = lax.all_gather(text_kv, "seq", axis=1, tiled=True)
+    text_all = jnp.concatenate(
+        lax.all_to_all(jnp.stack([text_kv] * lax.axis_size("seq")), "seq", 0, 0), axis=1
+    )
     chosen = jnp.take(text_all, prompts, axis=0)
     arrived, filled = dispatch(patches, layout, local_images)
     slot_rows = arrived.reshape(local_images * slot_span, arrived.shape[2])

time: 274 us -> 348 us (1.27)
  waiting for transfers between devices: 138 us -> 215 us
  blocking collectives: 39.6 us -> 6.77 us
  starting transfers between devices: 13.3 us -> 31.8 us
  local copies, waits for them, and re-layouts: 35.6 us -> 46.5 us
    all_to_all x0 -> x2, waiting for transfers between devices: none -> 96.3 us  [the longest x1 74.7 us: shards(): lax.all_to_all(jnp.stack([text_kv] * lax.axis_size('seq')), 'seq', 0, 0)]
    all_to_all x1 -> x0, blocking collectives: 32.8 us -> none  [dispatch(): lax.all_to_all(buffer, 'seq', split_axis=1, concat_axis=1, tiled=True)]
    all_gather x1 -> x0, waiting for transfers between devices: 30.5 us -> none  [shards(): text_all = lax.all_gather(text_kv, 'seq', axis=1, tiled=True)]
    all_to_all x0 -> x2, starting transfers between devices: none -> 11.8 us  [the longest x1 7.23 us: dispatch(): lax.all_to_all(buffer, 'seq', split_axis=1, concat_axis=1, tiled=True)]
    all_gather x1, waiting for transfers between devices: 21.8 us -> 31.3 us  [project(): gathered = lax.all_gather(row_data, 'mp', axis=1, tiled=True)]
    all_to_all x1, starting transfers between devices: 3.37 us -> 9.98 us  [dispatch(): lax.all_to_all(filled.reshape(local_images, slot_span), 'seq', split_axis...]
    all_to_all x0 -> x1, local copies, waits for them, and re-layouts: none -> 6.56 us  [shards(): lax.all_to_all(jnp.stack([text_kv] * lax.axis_size('seq')), 'seq', 0, 0)]
  transfers between devices with their start and end apart: 5 -> 6, of which waited for: 4 -> 5; matrix products, arithmetic and copies ran while one was open for 12% -> 12% of each run, Pallas kernels for 0% -> 0%
where the time goes in v1:
time: 348 us; the launch traced here: 347 us
  waiting for transfers between devices  215 us (62%)
  local copies, waits for them, and re-layouts  46.5 us (13%)
  starting transfers between devices  31.8 us (9%)
  matrix products  17.1 us (5%)
  other arithmetic  16.4 us (5%)
  between operations  13.7 us (4%)
  blocking collectives  6.77 us (2%)
    all_to_all x1, waiting for transfers between devices, shards(): lax.all_to_all(jnp.stack([text_kv] * lax.axis_size('seq')), 'seq', 0, 0)  74.7 us
    reduce_scatter x1, waiting for transfers between devices, finish(): lax.psum_scatter(partial_sum, 'mp', scatter_dimension=1, tiled=True)  64.4 us
    all_gather x1, waiting for transfers between devices, project(): gathered = lax.all_gather(row_data, 'mp', axis=1, tiled=True)  31.3 us
    all_to_all x1, waiting for transfers between devices, collect(): lax.all_to_all(slot_data, 'seq', split_axis=1, concat_axis=1, tiled=True)  22.7 us
    all_to_all x1, waiting for transfers between devices, dispatch(): lax.all_to_all(buffer, 'seq', split_axis=1, concat_axis=1, tiled=True)  21.6 us
    unnamed x33, local copies, waits for them, and re-layouts  13.8 us
    all_to_all x1, starting transfers between devices, dispatch(): lax.all_to_all(filled.reshape(local_images, slot_span), 'seq', split_axis...  9.98 us
    all_to_all x1, starting transfers between devices, collect(): lax.all_to_all(slot_data, 'seq', split_axis=1, concat_axis=1, tiled=True)  9.8 us
  transfers between devices with their start and end apart: 6, of which 5 were waited for; matrix products, arithmetic and copies ran while one was open for 12% of the time, Pallas kernels for 0%

profile of v1, /device:TPU:1, one launch (start us, length us, event | category | flops | bytes accessed | tf_op | source)
XLA Modules:
  0.0 347.0 jit_solution(14787336518948027935)
XLA Ops:
  9.0 1.2 compare_and_fusion.2
  10.2 2.2 scatter_custom_fusion.1
  13.1 10.0 %all-to-all-start.2 = ((bf16[2,16,16]{2,0,1:T(2,128)(2,1)}), bf16[2,16,16]{2,0,1:T(2,128)(2,1)S(1)}, u32[]{:S(2)}, u32[]{:S(2)}) async-start(bf16[2,16,16]{2,0,1:T(2,128)(2,1)} %copy.80), calls=%async_computation.2 | async-start | bytes 16384 | tf_op jit(solution)/shard_map/all_to_all | solution.py:48
  23.0 1.4 scatter_custom_fusion
  24.9 3.4 gather_fusion
  28.3 2.3 fusion.20
  30.7 7.2 %all-to-all-start = ((bf16[2,256,768]{2,0,1:T(2,128)(2,1)}), bf16[2,256,768]{2,0,1:T(2,128)(2,1)S(1)}, u32[]{:S(2)}, u32[]{:S(2)}) async-start(bf16[2,256,768]{2,0,1:T(2,128)(2,1)} %fusion.20), calls=%async_computation | async-start | bytes 1572864 | tf_op jit(solution)/shard_map/all_to_all | solution.py:47
  37.9 1.0 copy.77
  38.9 21.6 %all-to-all-done = bf16[2,256,768]{2,0,1:T(2,128)(2,1)S(1)} async-done(((bf16[2,256,768]{2,0,1:T(2,128)(2,1)}), bf16[2,256,768]{2,0,1:T(2,128)(2,1)S(1)}, u32[]{:S(2)}, u32[]{:S(2)}) %all-to-all-start) | async-done | bytes 786464 | tf_op jit(solution)/shard_map/all_to_all | solution.py:47
  60.5 3.4 stack.2
  64.0 4.5 %all-to-all-start.1 = ((bf16[16,16,16,2,384]{4,2,3,1,0:T(8,128)(2,1)}), bf16[16,16,16,2,384]{4,2,3,1,0:T(8,128)(2,1)}, u32[]{:S(2)}, u32[]{:S(2)}) async-start(bf16[16,16,16,2,384]{4,2,3,1,0:T(8,128)(2,1)} %stack.2), calls=%async_computation.1 | async-start | bytes 12582912 | tf_op jit(solution)/shard_map/all_to_all | solution.py:140
  68.5 1.0 copy.74
  69.8 10.3 %copy.75 = bf16[3072,3,384]{0,2,1:T(8,128)(2,1)} copy(bf16[3072,3,384]{2,0,1:T(8,128)(2,1)} %param.16) | data formatting | bytes 14155776 | tf_op args[5]
  81.6 31.3 %all-gather.2.cloned.1.call-done = bf16[512,3072]{1,0:T(8,128)(2,1)} async-done(((bf16[512,768]{1,0:T(8,128)(2,1)}), bf16[512,3072]{1,0:T(8,128)(2,1)}) %all-gather.2.cloned.1.call-update) | async-done | bytes 3145744 | tf_op jit(solution)/shard_map/all_gather | solution.py:61
  112.9 2.5 convert_reduce_fusion
  116.8 7.7 %fusion.13 = bf16[512,1152]{1,0:T(8,128)(2,1)S(1)} fusion(bf16[3072,1152]{0,1:T(8,128)(2,1)} %bitcast.54, bf16[512,3072]{1,0:T(8,128)(2,1)S(1)} %copy-done.1, f32[3072]{0:T(1024)S(1)} %copy-done.10, f32[3072]{0:T(1024)S(1)} %copy-done.11, f32[512]{0:T(512)S(1)} %add_rsqrt_fusion.1, f32[512]{0:T(512)S(1)} %broadcast_multiply_fusion.1), kind=kOutput, calls=%fused_computation.21 | convolution fusion | flops 3633905664 | bytes 11431936 | tf_op jit(solution)/shard_map/dot_general | solution.py:64
  125.3 1.2 copy.98
  128.4 2.6 fusion.41
  131.0 74.7 %all-to-all-done.1 = bf16[16,16,16,2,384]{4,2,3,1,0:T(8,128)(2,1)} async-done(((bf16[16,16,16,2,384]{4,2,3,1,0:T(8,128)(2,1)}), bf16[16,16,16,2,384]{4,2,3,1,0:T(8,128)(2,1)}, u32[]{:S(2)}, u32[]{:S(2)}) %all-to-all-start.1) | async-done | bytes 6291488 | tf_op jit(solution)/shard_map/all_to_all | solution.py:140
  205.6 6.6 %copy.78 = bf16[16,16,16,2,384]{4,2,0,3,1:T(8,128)(2,1)} copy(bf16[16,16,16,2,384]{4,2,3,1,0:T(8,128)(2,1)} %all-to-all-done.1) | data formatting | bytes 12582912 | tf_op jit(solution)/shard_map/all_to_all | solution.py:140
  212.2 3.5 %gather_fusion.1 = bf16[2,256,2,384]{3,1,2,0:T(8,128)(2,1)S(1)} fusion(bf16[16,256,2,384]{3,1,2,0:T(8,128)(2,1)} %bitcast.53, s32[1024]{0:T(1024)S(1)} %pad_clamp_fusion.1), kind=kCustom, calls=%fused_computation.1 | custom fusion | bytes 1572872 | tf_op jit(solution)/shard_map/jit(_take)/gather | solution.py:142
  218.5 1.6 fusion.42
  221.8 4.5 %fusion.43 = f32[512,3072]{1,0:T(8,128)} fusion(bf16[512,384]{0,1:T(8,128)(2,1)S(1)} %bitcast.60, bf16[384,3072]{1,0:T(8,128)(2,1)S(1)} %copy-done), kind=kOutput, calls=%fused_computation.83 | convolution fusion | flops 1207959552 | bytes 9043968 | tf_op jit(solution)/shard_map/dot_general | solution.py:106
  227.9 64.4 %reduce-scatter.2.cloned.1.call-done = f32[512,768]{1,0:T(8,128)} async-done(((f32[512,3072]{1,0:T(8,128)}), f32[512,768]{1,0:T(8,128)}) %reduce-scatter.2.cloned.1.call-update) | async-done | bytes 1572880 | tf_op jit(solution)/shard_map/reduce_scatter | solution.py:112
  292.3 1.7 fusion.38
  294.0 6.8 %all-reduce = (f32[512]{0:T(512)S(1)}, f32[512]{0:T(512)S(1)}) all-reduce(f32[512]{0:T(512)S(1)} %get-tuple-element.6, f32[512]{0:T(512)S(1)} %get-tuple-element.5), channel_id=1, replica_groups=mesh['dp'=4,'seq'=16,'mp'=4] {'mp'}, use_global_device_ids=true, to_apply=%region_15.16 | all-reduce | flops 1024 | bytes 8192 | tf_op jit(solution)/shard_map/psum | solution.py:113
  300.8 1.8 add_convert_fusion
  302.6 1.7 copy.91
  304.4 9.8 %all-to-all-start.3 = ((bf16[2,256,768]{2,0,1:T(2,128)(2,1)}), bf16[2,256,768]{2,0,1:T(2,128)(2,1)}, u32[]{:S(2)}, u32[]{:S(2)}) async-start(bf16[2,256,768]{2,0,1:T(2,128)(2,1)} %copy.91), calls=%async_computation.4 | async-start | bytes 1572864 | tf_op jit(solution)/shard_map/all_to_all | solution.py:56
  314.2 22.7 %all-to-all-done.3 = bf16[2,256,768]{2,0,1:T(2,128)(2,1)} async-done(((bf16[2,256,768]{2,0,1:T(2,128)(2,1)}), bf16[2,256,768]{2,0,1:T(2,128)(2,1)}, u32[]{:S(2)}, u32[]{:S(2)}) %all-to-all-start.3) | async-done | bytes 786464 | tf_op jit(solution)/shard_map/all_to_all | solution.py:56
  336.9 1.2 copy.92
  338.1 1.2 gather_fusion.2
  (78 shorter events, 16.3 us)
Async XLA Ops:
  6.5 215.2 %copy-start = (bf16[384,3072]{1,0:T(8,128)(2,1)S(1)}, bf16[384,3072]{1,0:T(8,128)(2,1)}, u32[]{:S(2)}) copy-start(bf16[384,3072]{1,0:T(8,128)(2,1)} %param.17) | copy-start | bytes 7077892
  10.2 14.5 %copy-start.6 = (s32[256]{0:T(256)}, s32[256]{0:T(256)S(1)}, u32[]{:S(2)}) copy-start(s32[256]{0:T(256)S(1)} %get-tuple-element.10) | copy-start | bytes 3076
  13.1 17.6 %all-to-all-start.2 = ((bf16[2,16,16]{2,0,1:T(2,128)(2,1)}), bf16[2,16,16]{2,0,1:T(2,128)(2,1)S(1)}, u32[]{:S(2)}, u32[]{:S(2)}) async-start(bf16[2,16,16]{2,0,1:T(2,128)(2,1)} %copy.80), calls=%async_computation.2 | async-start | bytes 16384 | tf_op jit(solution)/shard_map/all_to_all | solution.py:48
  30.7 29.9 %all-to-all-start = ((bf16[2,256,768]{2,0,1:T(2,128)(2,1)}), bf16[2,256,768]{2,0,1:T(2,128)(2,1)S(1)}, u32[]{:S(2)}, u32[]{:S(2)}) async-start(bf16[2,256,768]{2,0,1:T(2,128)(2,1)} %fusion.20), calls=%async_computation | async-start | bytes 1572864 | tf_op jit(solution)/shard_map/all_to_all | solution.py:47
  64.0 141.7 %all-to-all-start.1 = ((bf16[16,16,16,2,384]{4,2,3,1,0:T(8,128)(2,1)}), bf16[16,16,16,2,384]{4,2,3,1,0:T(8,128)(2,1)}, u32[]{:S(2)}, u32[]{:S(2)}) async-start(bf16[16,16,16,2,384]{4,2,3,1,0:T(8,128)(2,1)} %stack.2), calls=%async_computation.1 | async-start | bytes 12582912 | tf_op jit(solution)/shard_map/all_to_all | solution.py:140
  68.5 44.4 %all-gather.2.cloned.1.call-start = ((), (), s32[]{:S(2)}) async-start(), calls=%async_computation.5 | async-start | bytes 3932160 | tf_op jit(solution)/shard_map/all_gather | solution.py:61
  69.5 10.5 %copy-start.13 = (s32[1,2]{1,0:T(1,128)S(1)}, s32[1,2]{1,0:T(1,128)}, u32[]{:S(2)}) copy-start(s32[1,2]{1,0:T(1,128)} %param.13) | copy-start | bytes 28
  69.6 10.5 %copy-start.12 = (s32[1,16]{1,0:T(1,128)S(1)}, s32[1,16]{1,0:T(1,128)}, u32[]{:S(2)}) copy-start(s32[1,16]{1,0:T(1,128)} %param.14) | copy-start | bytes 196
  69.6 222.8 %reduce-scatter.2.cloned.1.call-start = ((), (), s32[]{:S(2)}) async-start(), calls=%async_computation.6 | async-start | bytes 7864320 | tf_op jit(solution)/shard_map/reduce_scatter | solution.py:112
  112.9 2.8 copy-start.1
  112.9 3.8 %copy-start.10 = (f32[3072]{0:T(1024)S(1)}, f32[3072]{0:T(1024)}, u32[]{:S(2)}) copy-start(f32[3072]{0:T(1024)} %param.19) | copy-start | bytes 36868
  112.9 3.8 %copy-start.11 = (f32[3072]{0:T(1024)S(1)}, f32[3072]{0:T(1024)}, u32[]{:S(2)}) copy-start(f32[3072]{0:T(1024)} %param.18) | copy-start | bytes 36868
  212.2 6.3 %copy-start.9 = (pred[2,256]{1,0:T(4,128)(4,1)S(1)}, pred[2,256]{1,0:T(4,128)(4,1)}, u32[]{:S(2)}) copy-start(pred[2,256]{1,0:T(4,128)(4,1)} %iota_compare_fusion.2) | copy-start | bytes 1540
  217.5 3.0 copy-start.4
  218.5 1.6 copy-start.3
  218.5 2.0 copy-start.5
  226.3 74.5 %copy-start.2 = (bf16[2,256,768]{2,1,0:T(8,128)(2,1)S(1)}, bf16[2,256,768]{2,1,0:T(8,128)(2,1)}, u32[]{:S(2)}) copy-start(bf16[2,256,768]{2,1,0:T(8,128)(2,1)} %copy.74) | copy-start | bytes 2359300
  300.8 13.4 %copy-start.7 = (s32[256]{0:T(256)S(1)}, s32[256]{0:T(256)}, u32[]{:S(2)}) copy-start(s32[256]{0:T(256)} %copy-done.6) | copy-start | bytes 3076
  304.4 35.0 %copy-start.8 = (pred[256]{0:T(512)(128)(4,1)S(1)}, pred[256]{0:T(512)(128)(4,1)}, u32[]{:S(2)}) copy-start(pred[256]{0:T(512)(128)(4,1)} %get-tuple-element.9) | copy-start | bytes 772
  304.4 32.6 %all-to-all-start.3 = ((bf16[2,256,768]{2,0,1:T(2,128)(2,1)}), bf16[2,256,768]{2,0,1:T(2,128)(2,1)}, u32[]{:S(2)}, u32[]{:S(2)}) async-start(bf16[2,256,768]{2,0,1:T(2,128)(2,1)} %copy.91), calls=%async_computation.4 | async-start | bytes 1572864 | tf_op jit(solution)/shard_map/all_to_all | solution.py:56
Sparse Core Ops, SparseCore 0:
  71.1 41.7 all-gather.1
  226.4 65.8 reduce-scatter.1
